TPU v7x, 128 devices: a whole 4x4x4 slice. The times are simulated.
128 devices in a mesh: row: 8 (over z, x_hi), col: 16 (over x_lo, y, core).
Axes of the slice: x: 4 (x_hi: 2, x_lo: 2; x = x_hi * 2 + x_lo), y: 4, z: 4, core: 2. Of those that a mesh axis runs over, the one named last changes fastest.
Arguments:
- pair: bfloat16 [1024, 1024, 128], P('row', 'col'), may hold values from -6 to 6
- left_gate: bfloat16 [128, 128], replicated, may hold values from -0.5 to 0.5
- left_proj: bfloat16 [128, 128], replicated, may hold values from -0.5 to 0.5
- right_gate: bfloat16 [128, 128], replicated, may hold values from -0.5 to 0.5
- right_proj: bfloat16 [128, 128], replicated, may hold values from -0.5 to 0.5
- out_gate: bfloat16 [128, 128], replicated, may hold values from -0.5 to 0.5
- out_proj: bfloat16 [128, 128], replicated, may hold values from -0.5 to 0.5
Outputs:
- update: bfloat16 [1024, 1024, 128], P('row', 'col')
All inputs are finite; a program needn't handle non-finite values.
Results may differ from a plain program's by a relative error of at most 0.0078.
Values may be sent and summed in bfloat16 or wider, within the bound.
No kernel may reach another device: no remote copies, remote signals or barrier semaphores. Data moves between devices by JAX's collectives and lax.ppermute only.
A program may use at most 192 MiB of HBM per device.

v0:
```python
import jax
import jax.numpy as jnp
from jax import lax
from jax.sharding import PartitionSpec as P


def layer_norm(values):
    values = values.astype(jnp.float32)
    center = values - jnp.mean(values, axis=-1, keepdims=True)
    spread = jnp.mean(center * center, axis=-1, keepdims=True)
    return center * lax.rsqrt(spread + 1e-05)


def project(normed, weight):
    flat = normed.reshape(-1, normed.shape[-1])
    out = jnp.dot(flat, weight, preferred_element_type=jnp.float32)
    return out.reshape(normed.shape[:-1] + (weight.shape[1],))


def on_device(pair, left_gate, left_proj, right_gate, right_proj, out_gate, out_proj):
    normed = layer_norm(pair).astype(jnp.bfloat16)
    left = (jax.nn.sigmoid(project(normed, left_gate)) * project(normed, left_proj)).astype(
        jnp.bfloat16
    )
    right = (jax.nn.sigmoid(project(normed, right_gate)) * project(normed, right_proj)).astype(
        jnp.bfloat16
    )
    right_all = lax.all_gather(right, "row", axis=0, tiled=True)
    turned = lax.psum_scatter(
        jnp.einsum("ikc,jkc->jic", left, right_all, preferred_element_type=jnp.float32),
        "col",
        scatter_dimension=0,
        tiled=True,
    )
    mixed = jnp.transpose(turned, (1, 0, 2))
    mixed_norm = layer_norm(mixed).astype(jnp.bfloat16)
    gated = jax.nn.sigmoid(project(normed, out_gate)) * project(mixed_norm, out_proj)
    return gated.astype(jnp.bfloat16)


def solution(mesh):
    return jax.shard_map(
        on_device,
        mesh=mesh,
        in_specs=(P("row", "col", None), P(), P(), P(), P(), P(), P()),
        out_specs=P("row", "col", None),
        check_vma=False,
    )
```

profile of v0, /device:TPU:1, one launch (start us, length us, event | category | flops | bytes accessed | tf_op | source)
XLA Modules:
  0.0 631.3 jit_solution(12479155525128052718)
XLA Ops:
  6.5 0.0 copy-start
  6.5 0.0 all-gather.2.cloned.1.call-start
  6.5 2.8 convert_reduce_fusion
  9.3 0.1 copy.35
  9.4 0.1 copy.36
  9.5 4.0 fusion.2
  13.5 0.1 copy.37
  13.6 0.1 copy.38
  13.7 5.3 fusion.3
  19.0 0.0 copy-done
  19.0 0.0 copy-start.6
  19.0 2.4 fusion.9
  21.4 0.0 copy-done.6
  21.4 0.0 copy-start.4
  21.4 4.4 multiply_convert_fusion.3
  25.8 0.0 copy-start.7
  25.8 0.0 all-gather.2.cloned.1.call-update
  25.8 0.2 reduce-scatter.2.cloned.1.call-start
  26.1 0.0 copy-done.4
  26.1 2.4 fusion.6
  28.5 0.0 copy-done.7
  28.5 4.4 multiply_convert_fusion.2
  32.9 4.2 copy.45
  37.1 174.7 %all-gather.2.cloned.1.call-done = bf16[1024,64,128]{2,0,1:T(8,128)(2,1)} async-done(((bf16[128,64,128]{2,0,1:T(8,128)(2,1)}), bf16[1024,64,128]{2,0,1:T(8,128)(2,1)}) %all-gather.2.cloned.1.call-update) | async-done | bytes 16777232 | tf_op jit(solution)/shard_map/all_gather | solution.py:28
  211.7 23.5 %copy.44 = bf16[1024,64,128]{0,1,2:T(8,128)(2,1)} copy(bf16[1024,64,128]{2,0,1:T(8,128)(2,1)} %all-gather.2.cloned.1.call-done) | data formatting | bytes 33554432 | tf_op jit(solution)/shard_map/all_gather | solution.py:28
  235.3 29.5 %convolution_bitcast_fusion = f32[1024,128,128]{1,0,2:T(8,128)} fusion(bf16[1024,64,128]{0,1,2:T(8,128)(2,1)} %copy.44, bf16[128,64,128]{0,1,2:T(8,128)(2,1)} %copy.45), kind=kOutput, calls=%fused_computation | convolution fusion | flops 2147483648 | bytes 85983232 | tf_op jit(solution)/shard_map/ikc,jkc->jic/dot_general | solution.py:30
  264.8 0.0 copy-start.5
  264.8 0.0 reduce-scatter.2.cloned.1.call-update
  264.8 0.7 copy-done.5
  265.5 4.3 fusion.11
  269.9 342.8 %reduce-scatter.2.cloned.1.call-done = f32[64,128,128]{1,0,2:T(8,128)} async-done(((f32[1024,128,128]{1,0,2:T(8,128)}), f32[64,128,128]{1,0,2:T(8,128)}) %reduce-scatter.2.cloned.1.call-update) | async-done | bytes 4194320 | tf_op jit(solution)/shard_map/reduce_scatter | solution.py:29
  612.7 0.0 copy-start.2
  612.7 2.6 bitcast_reduce_fusion
  615.3 0.8 copy-done.2
  616.2 0.5 multiply_reduce_fusion
  616.6 0.0 copy-start.3
  616.6 0.0 copy-start.8
  616.7 0.6 multiply_convert_fusion.1
  617.3 1.5 copy-done.3
  618.8 0.0 copy-done.8
  618.8 0.0 copy-start.1
  618.8 3.0 multiply_convert_fusion
  621.8 2.7 copy.47
  624.5 0.0 copy-done.1
  (4 shorter events, 0.1 us)
Async XLA Ops:
  6.5 12.5 %copy-start = (bf16[128,128]{1,0:T(8,128)(2,1)S(1)}, bf16[128,128]{1,0:T(8,128)(2,1)}, u32[]{:S(2)}) copy-start(bf16[128,128]{1,0:T(8,128)(2,1)} %param.10) | copy-start | bytes 98308
  6.5 205.2 %all-gather.2.cloned.1.call-start = ((), (), s32[]{:S(2)}) async-start(), calls=%async_computation.1 | async-start | bytes 18874368 | tf_op jit(solution)/shard_map/all_gather | solution.py:28
  19.0 2.4 copy-start.6
  21.4 4.6 copy-start.4
  25.8 2.7 copy-start.7
  25.8 586.9 %reduce-scatter.2.cloned.1.call-start = ((), (), s32[]{:S(2)}) async-start(), calls=%async_computation.2 | async-start | bytes 71303168 | tf_op jit(solution)/shard_map/reduce_scatter | solution.py:29
  264.8 0.8 copy-start.5
  612.7 3.4 copy-start.2
  616.6 2.2 copy-start.3
  616.6 2.2 copy-start.8
  618.8 5.7 copy-start.1
Sparse Core Ops, SparseCore 0:
  26.0 185.7 all-gather.1
  264.9 347.7 reduce-scatter.1
where the time goes:
time: 633 us; the launch traced here: 631 us
  waiting for transfers between devices  518 us (82%)
  matrix products  50.5 us (8%)
  local copies, waits for them, and re-layouts  33.7 us (5%)
  other arithmetic  15.8 us (2%)
  between operations  13.5 us (2%)
    reduce_scatter x1, waiting for transfers between devices, on_device(): lax.psum_scatter(jnp.einsum('ikc,jkc->jic', left, right_all, preferred_el...  343 us
    all_gather x1, waiting for transfers between devices, on_device(): right_all = lax.all_gather(right, 'row', axis=0, tiled=True)  175 us
    dot_general x1, matrix products, on_device(): jnp.einsum('ikc,jkc->jic', left, right_all, preferred_element_type=jnp.fl...  29.5 us
    all_gather x1, local copies, waits for them, and re-layouts, on_device(): right_all = lax.all_gather(right, 'row', axis=0, tiled=True)  23.5 us
    dot_general x6, matrix products, project(): out = jnp.dot(flat, weight, preferred_element_type=jnp.float32)  20.9 us
  transfers between devices with their start and end apart: 2, of which 2 were waited for; matrix products, arithmetic and copies ran while one was open for 2% of the time, Pallas kernels for 0%

commit v1 on v0

v1 whole, which is shorter than its diff:
```python
import jax
import jax.numpy as jnp
from jax import lax
from jax.experimental import pallas as pl
from jax.experimental.pallas import tpu as pltpu
from jax.sharding import PartitionSpec as P

C = 128
F32 = jnp.float32
BF16 = jnp.bfloat16
VMEM = 60 * 1024 * 1024

NT = (((1,), (1,)), ((), ()))
TN = (((0,), (0,)), ((), ()))


def sigmoid(x):
    return 0.5 * jnp.tanh(0.5 * x) + 0.5


def norm_rows(x):
    x = x.astype(F32)
    center = x - jnp.mean(x, axis=-1, keepdims=True)
    spread = jnp.mean(center * center, axis=-1, keepdims=True)
    return (center * lax.rsqrt(spread + 1e-05)).astype(BF16)


def edges_kernel(x_ref, lg_ref, lp_ref, rg_ref, rp_ref, o_ref, w_ref, stage):
    @pl.when(pl.program_id(0) == 0)
    def _():
        for n, ref in enumerate((lg_ref, lp_ref, rg_ref, rp_ref)):
            w_ref[n * C : (n + 1) * C, :] = ref[...].T

    steps = x_ref.shape[1]
    for s in range(0, steps, 2):
        x = jnp.concatenate(
            [x_ref[0, s], x_ref[1, s], x_ref[0, s + 1], x_ref[1, s + 1]], axis=0
        )
        p = lax.dot_general(w_ref[...], norm_rows(x), NT, preferred_element_type=F32)
        for side in range(2):
            at = 2 * C * side
            edge = sigmoid(p[at : at + C]) * p[at + C : at + 2 * C]
            stage[:, side, s, :] = edge[:, :C]
            stage[:, side, s + 1, :] = edge[:, C:]
    o_ref[...] = stage[...].astype(BF16)


def edges(pair4, lg, lp, rg, rp):
    _, steps, cols, ch = pair4.shape
    block = 16
    whole = pl.BlockSpec((C, C), lambda n: (0, 0))
    return pl.pallas_call(
        edges_kernel,
        grid=(steps // block,),
        in_specs=[pl.BlockSpec((2, block, cols, ch), lambda n: (0, n, 0, 0))] + [whole] * 4,
        out_specs=pl.BlockSpec((C, 2, block, 2 * cols), lambda n: (0, 0, n, 0)),
        out_shape=jax.ShapeDtypeStruct((C, 2, steps, 2 * cols), BF16),
        scratch_shapes=[
            pltpu.VMEM((4 * C, C), BF16),
            pltpu.VMEM((C, 2, block, 2 * cols), F32),
        ],
        compiler_params=pltpu.CompilerParams(vmem_limit_bytes=VMEM),
        cost_estimate=pl.CostEstimate(
            flops=2 * 4 * C * C * 8192, bytes_accessed=6 << 20, transcendentals=2 << 20
        ),
        name="edges",
    )(pair4, lg, lp, rg, rp)


def gate_kernel(x_ref, w_ref, o_ref):
    n = x_ref.shape[0]
    rows = x_ref.shape[1]
    for i in range(0, n, 4):
        x = x_ref[i : i + 4].reshape(4 * rows, C)
        p = jnp.dot(norm_rows(x), w_ref[...], preferred_element_type=F32)
        o_ref[i : i + 4] = sigmoid(p).reshape(4, rows, C)


def out_gates(pair, w):
    rows, cols, ch = pair.shape
    block = 16
    return pl.pallas_call(
        gate_kernel,
        grid=(rows // block,),
        in_specs=[
            pl.BlockSpec((block, cols, ch), lambda n: (n, 0, 0)),
            pl.BlockSpec((C, C), lambda n: (0, 0)),
        ],
        out_specs=pl.BlockSpec((block, cols, ch), lambda n: (n, 0, 0)),
        out_shape=jax.ShapeDtypeStruct((rows, cols, ch), F32),
        compiler_params=pltpu.CompilerParams(vmem_limit_bytes=VMEM),
        cost_estimate=pl.CostEstimate(
            flops=2 * C * C * 8192, bytes_accessed=6 << 20, transcendentals=1 << 20
        ),
        name="out_gates",
    )(pair, w)


def turn(top, low):
    h = top.shape[1] // 2
    return (
        jnp.concatenate([top[:, :h], low[:, :h]], axis=1),
        jnp.concatenate([top[:, h:], low[:, h:]], axis=1),
    )


def mix_kernel(l_ref, r_ref, o_ref, left, right):
    def gather(src, dst):
        rows, cols = src.shape[0], src.shape[1]
        s = src.shape[3]
        for r in range(rows):
            for q in range(0, cols, 2):
                a, b = turn(src[r, q, 0], src[r, q + 1, 0])
                dst[2 * r * s : 2 * r * s + s, q * s : q * s + 2 * s] = a
                dst[2 * r * s + s : 2 * r * s + 2 * s, q * s : q * s + 2 * s] = b

    @pl.when(pl.program_id(0) == 0)
    def _():
        gather(l_ref, left)

    gather(r_ref, right)
    s = o_ref.shape[2]
    for r in range(o_ref.shape[0]):
        m = lax.dot_general(
            left[2 * r * s : 2 * r * s + 2 * s, :], right[...], NT, preferred_element_type=F32
        ).astype(BF16)
        for q in range(0, o_ref.shape[1], 2):
            a, b = turn(m[:s, q * s : q * s + 2 * s], m[s:, q * s : q * s + 2 * s])
            o_ref[r, q] = a
            o_ref[r, q + 1] = b


def mix(got, rows, cols):
    steps, lanes = got.shape[2], got.shape[3]
    got = got.reshape(rows, cols, 2, steps, lanes)
    blocks = 4
    return pl.pallas_call(
        mix_kernel,
        grid=(blocks,),
        in_specs=[
            pl.BlockSpec((rows, cols, 1, steps, lanes), lambda n: (0, 0, 0, 0, 0)),
            pl.BlockSpec((rows // blocks, cols, 1, steps, lanes), lambda n: (n, 0, 1, 0, 0)),
        ],
        out_specs=pl.BlockSpec((rows, cols // blocks, steps, lanes), lambda n: (0, n, 0, 0)),
        out_shape=jax.ShapeDtypeStruct((rows, cols, steps, lanes), BF16),
        scratch_shapes=[
            pltpu.VMEM((2 * rows * steps, cols * steps), BF16),
            pltpu.VMEM((2 * rows * steps // blocks, cols * steps), BF16),
        ],
        compiler_params=pltpu.CompilerParams(vmem_limit_bytes=VMEM),
        cost_estimate=pl.CostEstimate(
            flops=2 << 30, bytes_accessed=6 << 20, transcendentals=0
        ),
        name="mix",
    )(got, got).reshape(rows * cols, steps, lanes)


def update_kernel(m_ref, g_ref, w_ref, o_ref, stage):
    m = m_ref[...].astype(F32)
    center = m - jnp.mean(m, axis=0, keepdims=True)
    spread = jnp.mean(center * center, axis=0, keepdims=True)
    stage[...] = center * lax.rsqrt(spread + 1e-05)
    cols = o_ref.shape[2]
    for s in range(m_ref.shape[1]):
        x = stage[:, s, :].astype(BF16)
        p = lax.dot_general(x, w_ref[...], TN, preferred_element_type=F32)
        o_ref[0, s] = (p[:cols] * g_ref[0, s]).astype(BF16)
        o_ref[1, s] = (p[cols:] * g_ref[1, s]).astype(BF16)


def update(mixed, gate4, w):
    _, steps, cols, ch = gate4.shape
    block = 16
    spec = pl.BlockSpec((2, block, cols, ch), lambda n: (0, n, 0, 0))
    return pl.pallas_call(
        update_kernel,
        grid=(steps // block,),
        in_specs=[
            pl.BlockSpec((C, block, 2 * cols), lambda n: (0, n, 0)),
            spec,
            pl.BlockSpec((C, C), lambda n: (0, 0)),
        ],
        out_specs=spec,
        out_shape=jax.ShapeDtypeStruct((2, steps, cols, ch), BF16),
        scratch_shapes=[pltpu.VMEM((C, block, 2 * cols), F32)],
        compiler_params=pltpu.CompilerParams(vmem_limit_bytes=VMEM),
        cost_estimate=pl.CostEstimate(
            flops=2 * C * C * 8192, bytes_accessed=8 << 20, transcendentals=0
        ),
        name="update",
    )(mixed, gate4, w)


def on_device(rows, cols, pair, left_gate, left_proj, right_gate, right_proj, out_gate, out_proj):
    ni, nj, ch = pair.shape
    pair4 = pair.reshape(2, ni // 2, nj, ch)
    sent = edges(pair4, left_gate, left_proj, right_gate, right_proj)
    got = lax.all_to_all(sent, ("row", "col"), 0, 0, tiled=True)
    gate = out_gates(pair, out_gate)
    mixed = mix(got, rows, cols)
    mixed = lax.all_to_all(mixed, ("row", "col"), 0, 0, tiled=True)
    out = update(mixed, gate.reshape(2, ni // 2, nj, ch), out_proj)
    return out.reshape(ni, nj, ch)


def solution(mesh):
    rows, cols = mesh.shape["row"], mesh.shape["col"]

    def body(*args):
        return on_device(rows, cols, *args)

    return jax.shard_map(
        body,
        mesh=mesh,
        in_specs=(P("row", "col", None), P(), P(), P(), P(), P(), P()),
        out_specs=P("row", "col", None),
        check_vma=False,
    )
```

time: 633 us -> 133 us (0.21)
  waiting for transfers between devices: 518 us -> 22.9 us
  blocking collectives: 0 us -> 64.8 us
  matrix products: 50.5 us -> 0 us
  Pallas kernels: 0 us -> 39.2 us
  local copies, waits for them, and re-layouts: 33.7 us -> 1.32 us
  other arithmetic: 15.8 us -> 0 us
  between operations: 13.5 us -> 0.01 us
    reduce_scatter x1 -> x0, waiting for transfers between devices: 343 us -> none  [on_device(): lax.psum_scatter(jnp.einsum('ikc,jkc->jic', left, right_all, preferred_el...]
    all_gather x1 -> x0, waiting for transfers between devices: 175 us -> none  [on_device(): right_all = lax.all_gather(right, 'row', axis=0, tiled=True)]
    all_to_all x0 -> x1, blocking collectives: none -> 64.8 us  [on_device(): got = lax.all_to_all(sent, ('row', 'col'), 0, 0, tiled=True)]
    dot_general x7 -> x0, matrix products: 50.5 us -> none  [the longest x1 29.5 us: on_device(): jnp.einsum('ikc,jkc->jic', left, right_all, preferred_element_type=jnp.fl...]
    pallas_call x0 -> x4, Pallas kernels: none -> 39.2 us  [the longest x1 11.7 us: edges(): pl.pallas_call(edges_kernel, grid=(steps // block,), in_specs=[pl.BlockSp...]
    all_gather x1 -> x0, local copies, waits for them, and re-layouts: 23.5 us -> none  [on_device(): right_all = lax.all_gather(right, 'row', axis=0, tiled=True)]
    all_to_all x0 -> x1, waiting for transfers between devices: none -> 22.9 us  [on_device(): mixed = lax.all_to_all(mixed, ('row', 'col'), 0, 0, tiled=True)]
    reduce_sum x4 -> x0, other arithmetic: 9.86 us -> none  [the longest x2 5.36 us: layer_norm(): center = values - jnp.mean(values, axis=-1, keepdims=True)]
  transfers between devices with their start and end apart: 2 -> 1, of which waited for: 2 -> 1; matrix products, arithmetic and copies ran while one was open for 2% -> 0% of each run, Pallas kernels for 0% -> 6%
where the time goes in v1:
time: 133 us; the launch traced here: 132 us
  blocking collectives  64.8 us (49%)
  Pallas kernels  39.2 us (29%)
  waiting for transfers between devices  22.9 us (17%)
  starting transfers between devices  4.29 us (3%)
    all_to_all x1, blocking collectives, on_device(): got = lax.all_to_all(sent, ('row', 'col'), 0, 0, tiled=True)  64.8 us
    all_to_all x1, waiting for transfers between devices, on_device(): mixed = lax.all_to_all(mixed, ('row', 'col'), 0, 0, tiled=True)  22.9 us
    pallas_call x1, Pallas kernels, edges(): pl.pallas_call(edges_kernel, grid=(steps // block,), in_specs=[pl.BlockSp...  11.7 us
    pallas_call x1, Pallas kernels, mix(): pl.pallas_call(mix_kernel, grid=(blocks,), in_specs=[pl.BlockSpec((rows,...  9.96 us
    pallas_call x1, Pallas kernels, update(): pl.pallas_call(update_kernel, grid=(steps // block,), in_specs=[pl.BlockS...  9.76 us
    pallas_call x1, Pallas kernels, out_gates(): pl.pallas_call(gate_kernel, grid=(rows // block,), in_specs=[pl.BlockSpec...  7.78 us
    all_to_all x1, starting transfers between devices, on_device(): mixed = lax.all_to_all(mixed, ('row', 'col'), 0, 0, tiled=True)  4.29 us
  transfers between devices with their start and end apart: 1, of which 1 were waited for; matrix products, arithmetic and copies ran while one was open for 0% of the time, Pallas kernels for 6%

profile of v1, /device:TPU:1, one launch (start us, length us, event | category | flops | bytes accessed | tf_op | source)
XLA Modules:
  0.0 132.5 jit_solution(4314951763410929404)
XLA Ops:
  0.0 11.7 %edges.1 = bf16[128,2,64,128]{3,2,1,0:T(8,128)(2,1)} custom-call(bf16[2,64,64,128]{3,2,1,0:T(8,128)(2,1)} %bitcast.8, bf16[128,128]{1,0:T(8,128)(2,1)} %lg_ref.1, bf16[128,128]{1,0:T(8,128)(2,1)} %lp_ref.1, bf16[128,128]{1,0:T(8,128)(2,1)} %rg_ref.1, bf16[128,128]{1,0:T(8,128)(2,1)} %rp_ref.1), custom_call_target="tpu_custom_call" | custom-call | flops 1073741824 | bytes 6291456 | tf_op jit(solution)/shard_map/edges/pallas_call | solution.py:52
  11.7 64.8 %all_to_all.10 = bf16[128,2,64,128]{3,2,1,0:T(8,128)(2,1)} all-to-all(bf16[128,2,64,128]{3,2,1,0:T(8,128)(2,1)} %edges.1), channel_id=1, replica_groups=mesh['row'=8,'col'=16] {'row','col'}, dimensions={0} | all-to-all | bytes 8388608 | tf_op jit(solution)/shard_map/all_to_all | solution.py:198
  76.5 10.0 %mix.1 = bf16[8,16,64,128]{3,2,1,0:T(8,128)(2,1)} custom-call(bf16[8,16,2,64,128]{4,3,2,1,0:T(8,128)(2,1)} %bitcast.5, bf16[8,16,2,64,128]{4,3,2,1,0:T(8,128)(2,1)} %bitcast.6), custom_call_target="tpu_custom_call" | custom-call | flops 2147483648 | bytes 6291456 | tf_op jit(solution)/shard_map/mix/pallas_call | solution.py:137
  86.4 4.3 %all-to-all-start.1 = ((bf16[128,64,128]{2,1,0:T(8,128)(2,1)}), bf16[128,64,128]{2,1,0:T(8,128)(2,1)S(1)}, u32[]{:S(2)}, u32[]{:S(2)}) async-start(bf16[128,64,128]{2,1,0:T(8,128)(2,1)} %bitcast.9), calls=%async_computation.1 | async-start | bytes 4194304 | tf_op jit(solution)/shard_map/all_to_all | solution.py:201
  90.7 7.8 %out_gates.1 = f32[128,64,128]{2,1,0:T(8,128)} custom-call(bf16[128,64,128]{2,1,0:T(8,128)(2,1)} %x_ref.1, bf16[128,128]{1,0:T(8,128)(2,1)} %w_ref.2), custom_call_target="tpu_custom_call" | custom-call | flops 268435456 | bytes 6291456 | tf_op jit(solution)/shard_map/out_gates/pallas_call | solution.py:82
  98.5 22.9 %all-to-all-done.1.m_ref = bf16[128,64,128]{2,1,0:T(8,128)(2,1)S(1)} async-done(((bf16[128,64,128]{2,1,0:T(8,128)(2,1)}), bf16[128,64,128]{2,1,0:T(8,128)(2,1)S(1)}, u32[]{:S(2)}, u32[]{:S(2)}) %all-to-all-start.1) | async-done | bytes 2097184 | tf_op jit(solution)/shard_map/all_to_all | solution.py:201
  121.4 0.0 copy-start
  121.4 1.3 copy-done
  122.7 9.8 %update.1 = bf16[2,64,64,128]{3,2,1,0:T(8,128)(2,1)} custom-call(bf16[128,64,128]{2,1,0:T(8,128)(2,1)} %copy-done, f32[2,64,64,128]{3,2,1,0:T(8,128)} %bitcast.7, bf16[128,128]{1,0:T(8,128)(2,1)} %w_ref.3), custom_call_target="tpu_custom_call" | custom-call | flops 268435456 | bytes 8388608 | tf_op jit(solution)/shard_map/update/pallas_call | solution.py:175
Async XLA Ops:
  86.4 35.0 %all-to-all-start.1 = ((bf16[128,64,128]{2,1,0:T(8,128)(2,1)}), bf16[128,64,128]{2,1,0:T(8,128)(2,1)S(1)}, u32[]{:S(2)}, u32[]{:S(2)}) async-start(bf16[128,64,128]{2,1,0:T(8,128)(2,1)} %bitcast.9), calls=%async_computation.1 | async-start | bytes 4194304 | tf_op jit(solution)/shard_map/all_to_all | solution.py:201
  121.4 1.3 copy-start
